TPU v7x, 256 devices: a whole 4x4x8 slice. The times are simulated.
256 devices in a mesh: dom: 64 (over y, x, z_hi, core), row: 4 (over z_lo).
Axes of the slice: x: 4, y: 4, z: 8 (z_hi: 2, z_lo: 4; z = z_hi * 4 + z_lo), core: 2. Of those that a mesh axis runs over, the one named last changes fastest.
Arguments:
- state: float32 [3, 64, 64, 4096], P(None, 'dom', 'row'), may hold values from -1.5 to 3, as said below
- rain: float32 [64, 64, 4096], P('dom', 'row'), may hold values from 0 to 0.5
- ground: float32 [64, 4096], P('row'), may hold values from 0 to 1
- counts: int32 [64], replicated, may hold values from 0 to 16, as said below
- slot_map: int32 [64], replicated, may hold values from 0 to 63, each once
Outputs:
- resampled: float32 [3, 64, 64, 4096], P(None, 'dom', 'row')
Inputs may be any that keep to these rules, and one draw needn't show every extreme that they name: `state`: depth (component 0) lies in 0.5 to 3; both momenta (components 1 and 2) lie in -1.5 to 1.5. counts sum to 64; one particle gets exactly 16 copies, others at most 2, many none. `slot_map`: each slot appears once.
All inputs are finite; a program needn't handle non-finite values.
Results may differ from a plain program's by a relative error of at most 0.00002.
Values sent between devices are 32-bit elements; how exact they have to be, the bound alone decides.
No kernel may reach another device: no remote copies, remote signals or barrier semaphores. Data moves between devices by JAX's collectives and lax.ppermute only.
A program may use at most 192 MiB of HBM per device.

v0:
```python
import jax
import jax.numpy as jnp
from jax import lax
from jax.sharding import PartitionSpec as P

gravity = 9.81
courant = 0.04


def with_halo(block, sides, width):
    for axis, dim in sides:
        count = lax.axis_size(axis)
        forward = [(i, i + 1) for i in range(count - 1)]
        backward = [(target, source) for source, target in forward]
        low = lax.ppermute(
            lax.slice_in_dim(block, block.shape[dim] - width, None, axis=dim), axis, forward
        )
        high = lax.ppermute(lax.slice_in_dim(block, 0, width, axis=dim), axis, backward)
        block = jnp.concatenate([low, block, high], axis=dim)
    return block


def hll_flux(depth_l, norm_l, tang_l, depth_r, norm_r, tang_r):
    vel_l = norm_l / depth_l
    vel_r = norm_r / depth_r
    cel_l = jnp.sqrt(gravity * depth_l)
    cel_r = jnp.sqrt(gravity * depth_r)
    lower = jnp.minimum(jnp.minimum(vel_l - cel_l, vel_r - cel_r), 0.0)
    upper = jnp.maximum(jnp.maximum(vel_l + cel_l, vel_r + cel_r), 0.0)
    scale = 1.0 / (upper - lower)
    left_f = (norm_l, norm_l * vel_l + 0.5 * gravity * depth_l * depth_l, tang_l * vel_l)
    right_f = (norm_r, norm_r * vel_r + 0.5 * gravity * depth_r * depth_r, tang_r * vel_r)
    left_u = (depth_l, norm_l, tang_l)
    right_u = (depth_r, norm_r, tang_r)
    return tuple(
        (
            (upper * fl - lower * fr + upper * lower * (ur - ul)) * scale
            for fl, fr, ul, ur in zip(left_f, right_f, left_u, right_u)
        )
    )


def wall_cols(field, sign):
    return jnp.concatenate([field[:, :1] * sign, field, field[:, -1:] * sign], axis=1)


def advance(padded, rain_now):
    depth = wall_cols(padded[0], 1.0)
    flow_a = wall_cols(padded[1], 1.0)
    flow_b = wall_cols(padded[2], -1.0)
    bed = wall_cols(padded[3], 1.0)
    row_f = hll_flux(
        depth[:-1, 1:-1],
        flow_a[:-1, 1:-1],
        flow_b[:-1, 1:-1],
        depth[1:, 1:-1],
        flow_a[1:, 1:-1],
        flow_b[1:, 1:-1],
    )
    col_f = hll_flux(
        depth[1:-1, :-1],
        flow_b[1:-1, :-1],
        flow_a[1:-1, :-1],
        depth[1:-1, 1:],
        flow_b[1:-1, 1:],
        flow_a[1:-1, 1:],
    )
    depth_c = depth[1:-1, 1:-1]
    new_depth = (
        depth_c
        - courant * (row_f[0][1:] - row_f[0][:-1])
        - courant * (col_f[0][:, 1:] - col_f[0][:, :-1])
        + rain_now
    )
    new_a = (
        flow_a[1:-1, 1:-1]
        - courant * (row_f[1][1:] - row_f[1][:-1])
        - courant * (col_f[2][:, 1:] - col_f[2][:, :-1])
        - courant * gravity * depth_c * (bed[2:, 1:-1] - bed[:-2, 1:-1]) * 0.5
    )
    new_b = (
        flow_b[1:-1, 1:-1]
        - courant * (row_f[2][1:] - row_f[2][:-1])
        - courant * (col_f[1][:, 1:] - col_f[1][:, :-1])
        - courant * gravity * depth_c * (bed[1:-1, 2:] - bed[1:-1, :-2]) * 0.5
    )
    return jnp.stack([new_depth, new_a, new_b])


def ancestors_of(counts, slot_map):
    total = counts.shape[0]
    places = jnp.arange(total, dtype=jnp.int32)
    cumul = jnp.cumsum(counts)
    ordered = jnp.sum((cumul[None, :] <= places[:, None]).astype(jnp.int32), axis=1)
    hits = (slot_map[None, :] == places[:, None]).astype(jnp.int32)
    return jnp.sum(hits * ordered[None, :], axis=1)


def step_strip(fields, rain_now, ground):
    signs = jnp.array([1.0, -1.0, 1.0, 1.0], jnp.float32)[:, None, None]
    stacked = jnp.concatenate([fields, ground[None]], axis=0)
    padded = with_halo(stacked, (("row", 1),), 1)
    strip = lax.axis_index("row")
    top_row = jnp.where(strip == 0, padded[:, 1:2] * signs, padded[:, :1])
    low_row = jnp.where(strip == lax.axis_size("row") - 1, padded[:, -2:-1] * signs, padded[:, -1:])
    padded = jnp.concatenate([top_row, padded[:, 1:-1], low_row], axis=1)
    return advance(padded, rain_now)


def on_device(state, rain, ground, counts, slot_map):
    ancestor = ancestors_of(counts, slot_map)
    fields = state[:, 0]
    rows_dev = fields.shape[1]
    width = fields.shape[2]
    stepped = step_strip(fields, rain[0], ground)
    outgoing = stepped.reshape(1, 3, rows_dev * width)
    received = lax.all_to_all(outgoing, "dom", split_axis=2, concat_axis=0, tiled=True)
    chosen = received[ancestor]
    returned = lax.all_to_all(chosen, "dom", split_axis=0, concat_axis=2, tiled=True)
    result = returned.reshape(3, rows_dev, width)
    return result[:, None]


def solution(mesh):
    placed = (P(None, "dom", "row", None), P("dom", "row", None), P("row", None), P(), P())
    return jax.shard_map(
        on_device,
        mesh=mesh,
        in_specs=placed,
        out_specs=P(None, "dom", "row", None),
        check_vma=False,
    )
```

profile of v0, /device:TPU:33, one launch (start us, length us, event | category | flops | bytes accessed | tf_op | source)
XLA Modules:
  0.0 534.9 jit_solution(90363265837212891)
XLA Ops:
  0.0 0.0 copy-start.3
  0.0 0.0 copy-start
  0.0 1.2 pad_maximum_fusion.11
  1.2 3.5 collective-permute-start
  4.8 1.4 collective-permute-done
  6.2 0.0 copy-done
  6.2 1.0 broadcast_select_fusion.1
  7.3 1.9 collective-permute-start.1
  9.2 3.3 collective-permute-done.1
  12.5 0.0 copy-done.3
  12.5 0.1 broadcast_select_fusion
  12.6 0.0 copy-done.1
  12.6 0.2 pad_maximum_fusion.1
  12.9 0.3 maximum_maximum_fusion
  13.2 0.1 slice_bitcast_fusion.1
  13.3 0.7 fusion.41
  14.0 0.1 slice_multiply_fusion
  14.1 0.6 add_multiply_fusion.3
  14.7 0.5 add_multiply_fusion.2
  15.3 0.8 add_multiply_fusion.1
  16.1 0.0 copy-start.2
  16.1 0.2 fusion.27
  16.3 0.3 stack.13
  16.6 0.4 copy-done.2
  17.0 1.1 fusion.34
  18.1 0.3 stack.12
  18.5 0.3 stack.14
  18.8 0.7 pad_maximum_fusion.2
  19.5 47.6 %copy.37 = f32[1,3,65536]{1,0,2:T(1,128)} copy(f32[1,3,65536]{2,1,0:T(4,128)S(1)} %pad_maximum_fusion.2) | data formatting | bytes 1572864 | tf_op jit(solution)/shard_map/stack | solution.py:87
  67.1 0.6 broadcast.135
  67.7 291.0 %reduce.1 = f32[65536,3]{1,0:T(8,128)} reduce(f32[65536,1,3]{2,1,0:T(1,128)} %bitcast.144, f32[]{:T(128)} %broadcast.135), dimensions={1}, to_apply=%bitcast.142.reduce_sub_computation | reduce | bytes 1572868
  358.7 27.2 %reshape.79 = f32[64,1,3072]{2,1,0:T(1,128)} reshape(f32[65536,3]{1,0:T(8,128)} %reduce.1) | data formatting | bytes 1572864
  385.9 16.1 %all-to-all-start = ((f32[64,1,3072]{2,1,0:T(1,128)}), f32[64,1,3072]{2,1,0:T(1,128)S(1)}, u32[]{:S(2)}, u32[]{:S(2)}) async-start(f32[64,1,3072]{2,1,0:T(1,128)} %reshape.79), calls=%async_computation | async-start | bytes 1572864 | tf_op jit(solution)/shard_map/all_to_all | solution.py:117
  402.1 0.0 copy-done.4
  402.1 0.1 copy.40
  402.2 0.1 reduce-window.8
  402.3 0.1 reduce
  402.4 0.1 convert_reduce_fusion
  402.5 0.0 copy-done.5
  402.5 0.1 select_reduce_fusion
  402.6 26.8 %all-to-all-done = f32[64,1,3072]{2,1,0:T(1,128)S(1)} async-done(((f32[64,1,3072]{2,1,0:T(1,128)}), f32[64,1,3072]{2,1,0:T(1,128)S(1)}, u32[]{:S(2)}, u32[]{:S(2)}) %all-to-all-start) | async-done | bytes 786464 | tf_op jit(solution)/shard_map/all_to_all | solution.py:117
  429.4 2.6 reduce.2
  432.0 49.8 %reshape.80 = f32[65536,1,3]{2,1,0:T(1,128)} reshape(f32[64,3072]{1,0:T(8,128)S(1)} %reduce.2) | data formatting | bytes 1572864
  481.8 17.6 %copy.39 = f32[1,3,64,1024]{3,1,2,0:T(4,128)S(1)} copy(f32[1,3,64,1024]{1,3,2,0:T(8,128)} %bitcast.145) | data formatting | bytes 1572864 | tf_op jit(solution)/shard_map/all_to_all | solution.py:117
  499.4 1.2 gather_fusion
  500.6 32.6 %all_to_all.33 = f32[64,3,1024]{2,1,0:T(4,128)S(1)} all-to-all(f32[64,3,1024]{2,1,0:T(4,128)S(1)} %gather_fusion), channel_id=1, replica_groups=mesh['dom'=64,'row'=4] {'dom'}, dimensions={0} | all-to-all | bytes 1572864 | tf_op jit(solution)/shard_map/all_to_all | solution.py:119
  533.2 0.5 copy.41
  533.7 1.2 broadcast_in_dim_reshape.3
  (5 shorter events, 0.0 us)
Async XLA Ops:
  0.0 12.5 %copy-start.3 = (f32[4]{0:T(128)S(1)}, f32[4]{0:T(128)}, u32[]{:S(2)}) copy-start(f32[4]{0:T(128)} %constant.10.clone) | copy-start | bytes 52
  0.0 6.2 %copy-start = (f32[3,1,16,4096]{3,2,1,0:T(8,128)S(1)}, f32[3,1,16,4096]{3,2,1,0:T(8,128)}, u32[]{:S(2)}) copy-start(f32[3,1,16,4096]{3,2,1,0:T(8,128)} %param.6) | copy-start | bytes 2359300
  0.0 12.6 %copy-start.1 = (f32[16,4096]{1,0:T(8,128)S(1)}, f32[16,4096]{1,0:T(8,128)}, u32[]{:S(2)}) copy-start(f32[16,4096]{1,0:T(8,128)} %param.8) | copy-start | bytes 786436
  1.2 5.0 collective-permute-start
  7.3 5.2 collective-permute-start.1
  16.1 1.0 copy-start.2
  385.9 16.2 %copy-start.4 = (s32[64]{0:T(128)S(1)}, s32[64]{0:T(128)}, u32[]{:S(2)}) copy-start(s32[64]{0:T(128)} %param.9) | copy-start | bytes 772
  385.9 16.6 %copy-start.5 = (s32[64]{0:T(128)S(1)}, s32[64]{0:T(128)}, u32[]{:S(2)}) copy-start(s32[64]{0:T(128)} %param.10) | copy-start | bytes 772
  385.9 43.5 %all-to-all-start = ((f32[64,1,3072]{2,1,0:T(1,128)}), f32[64,1,3072]{2,1,0:T(1,128)S(1)}, u32[]{:S(2)}, u32[]{:S(2)}) async-start(f32[64,1,3072]{2,1,0:T(1,128)} %reshape.79), calls=%async_computation | async-start | bytes 1572864 | tf_op jit(solution)/shard_map/all_to_all | solution.py:117
where the time goes:
time: 536 us; the launch traced here: 535 us
  other arithmetic  301 us (56%)
  local copies, waits for them, and re-layouts  148 us (28%)
  blocking collectives  32.6 us (6%)
  waiting for transfers between devices  31.5 us (6%)
  starting transfers between devices  21.6 us (4%)
    unnamed x1, other arithmetic  291 us
    unnamed x15, local copies, waits for them, and re-layouts  78 us
    another operation x4, local copies, waits for them, and re-layouts, advance(): return jnp.stack([new_depth, new_a, new_b])  48.6 us
    all_to_all x1, blocking collectives, on_device(): lax.all_to_all(chosen, 'dom', split_axis=0, concat_axis=2, tiled=True)  32.6 us
    all_to_all x1, waiting for transfers between devices, on_device(): lax.all_to_all(outgoing, 'dom', split_axis=2, concat_axis=0, tiled=True)  26.8 us
    all_to_all x1, local copies, waits for them, and re-layouts, on_device(): lax.all_to_all(outgoing, 'dom', split_axis=2, concat_axis=0, tiled=True)  17.6 us
    all_to_all x1, starting transfers between devices, on_device(): lax.all_to_all(outgoing, 'dom', split_axis=2, concat_axis=0, tiled=True)  16.1 us
  transfers between devices with their start and end apart: 3, of which 3 were waited for; matrix products, arithmetic and copies ran while one was open for 0% of the time, Pallas kernels for 0%

commit v1 on v0

v1 whole, which is shorter than its diff:
```python
import functools

import jax
import jax.numpy as jnp
from jax import lax
from jax.experimental import pallas as pl
from jax.experimental.pallas import tpu as pltpu
from jax.sharding import Mesh, PartitionSpec as P

gravity = 9.81
courant = 0.04
LANES = 128
SUBLANES = 8


def cell_terms(depth, norm, tang):
    vel = norm / depth
    cel = jnp.sqrt(gravity * depth)
    press = 0.5 * gravity * depth * depth
    return depth, norm, tang, norm * vel + press, tang * vel, vel - cel, vel + cel


def interface(left, right):
    depth_l, norm_l, tang_l, fnorm_l, ftang_l, slow_l, fast_l = left
    depth_r, norm_r, tang_r, fnorm_r, ftang_r, slow_r, fast_r = right
    lower = jnp.minimum(jnp.minimum(slow_l, slow_r), 0.0)
    upper = jnp.maximum(jnp.maximum(fast_l, fast_r), 0.0)
    scale = 1.0 / (upper - lower)
    both = upper * lower
    return (
        (upper * norm_l - lower * norm_r + both * (depth_r - depth_l)) * scale,
        (upper * fnorm_l - lower * fnorm_r + both * (norm_r - norm_l)) * scale,
        (upper * ftang_l - lower * ftang_r + both * (tang_r - tang_l)) * scale,
    )


def both_ways(depth, flow_a, flow_b):
    inverse = 1.0 / depth
    cel = jnp.sqrt(gravity * depth)
    press = (0.5 * gravity) * depth * depth
    vel_a = flow_a * inverse
    vel_b = flow_b * inverse
    cross = flow_a * vel_b
    by_row = (depth, flow_a, flow_b, flow_a * vel_a + press, cross, vel_a - cel, vel_a + cel)
    by_col = (depth, flow_b, flow_a, flow_b * vel_b + press, cross, vel_b - cel, vel_b + cel)
    return by_row, by_col


def step_kernel(state_ref, rain_ref, ground_ref, out_ref):
    rows, width = ground_ref.shape
    tiles = width // LANES
    shape = (rows, LANES)
    lane = lax.broadcasted_iota(jnp.int32, shape, 1)
    row = lax.broadcasted_iota(jnp.int32, shape, 0)
    first_lane, last_lane = lane == 0, lane == LANES - 1
    first_row, last_row = row == 0, row == rows - 1

    def load(tile):
        at = pl.ds(pl.multiple_of(tile * LANES, LANES), LANES)
        return state_ref[0, 0, :, at], state_ref[1, 0, :, at], state_ref[2, 0, :, at], ground_ref[:, at]

    def rolled(terms):
        return tuple(pltpu.roll(term, LANES - 1, 1) for term in terms)

    def one(tile, carry):
        cells, bed, cells_r, bed_r, flux_before, bed_before = carry
        depth, flow_a, flow_b = cells[0]
        by_row, by_col = cells[1], cells[2]
        nxt = jnp.minimum(tile + 1, tiles - 1)
        n_depth, n_a, n_b, n_bed = load(nxt)
        n_row, n_col = both_ways(n_depth, n_a, n_b)
        n_rolled = rolled(n_col)
        n_bed_r = pltpu.roll(n_bed, LANES - 1, 1)
        right = tuple(jnp.where(last_lane, n, c) for n, c in zip(n_rolled, cells_r))
        at_wall = tile == tiles - 1
        ghost = jnp.logical_and(last_lane, at_wall)
        g_depth, g_norm, g_tang, g_fnorm, g_ftang, g_slow, g_fast = by_col
        mirror = (g_depth, -g_norm, g_tang, g_fnorm, -g_ftang, -g_fast, -g_slow)
        right = tuple(jnp.where(ghost, m, r) for m, r in zip(mirror, right))
        bed_next = jnp.where(ghost, bed, jnp.where(last_lane, n_bed_r, bed_r))
        flux = interface(by_col, right)
        flux_r = tuple(pltpu.roll(f, 1, 1) for f in flux)
        flux_left = tuple(jnp.where(first_lane, b, f) for b, f in zip(flux_before, flux_r))
        bed_rolled = pltpu.roll(bed, 1, 1)
        bed_left = jnp.where(first_lane, bed_before, bed_rolled)

        above = tuple(pltpu.roll(term, 1, 0) for term in by_row)
        inner = interface(above, by_row)
        inner = tuple(jnp.where(first_row, 0.0, f) for f in inner)
        below = tuple(pltpu.roll(f, rows - 1, 0) for f in inner)
        bed_up = jnp.where(first_row, 0.0, pltpu.roll(bed, 1, 0))
        bed_down = jnp.where(last_row, 0.0, pltpu.roll(bed, rows - 1, 0))

        pull = (0.5 * courant * gravity) * depth
        at = pl.ds(pl.multiple_of(tile * LANES, LANES), LANES)
        new_depth = depth - courant * ((below[0] - inner[0]) + (flux[0] - flux_left[0])) + rain_ref[0, :, at]
        new_a = flow_a - courant * ((below[1] - inner[1]) + (flux[2] - flux_left[2])) - pull * (bed_down - bed_up)
        new_b = flow_b - courant * ((below[2] - inner[2]) + (flux[1] - flux_left[1])) - pull * (bed_next - bed_left)
        for part, value in enumerate((new_depth, new_a, new_b)):
            for top in range(rows // SUBLANES):
                out_ref[tile, top, part] = value[top * SUBLANES : (top + 1) * SUBLANES]
        return ((n_depth, n_a, n_b), n_row, n_col), n_bed, n_rolled, n_bed_r, flux_r, bed_rolled

    depth, flow_a, flow_b, bed = load(0)
    by_row, by_col = both_ways(depth, flow_a, flow_b)
    g_depth, g_norm, g_tang, g_fnorm, g_ftang, g_slow, g_fast = by_col
    mirror = (g_depth, -g_norm, g_tang, g_fnorm, -g_ftang, -g_fast, -g_slow)
    start = (
        ((depth, flow_a, flow_b), by_row, by_col),
        bed,
        rolled(by_col),
        pltpu.roll(bed, LANES - 1, 1),
        interface(mirror, by_col),
        bed,
    )
    lax.fori_loop(0, tiles, one, start)


def edge_kernel(strip_ref, first_ref, last_ref, top_ref, low_ref, part_ref, out_ref, top_sc, low_sc, *, strips):
    strip = strip_ref[0]

    def fluxes(inside, outside, at_wall, upward):
        own = tuple(inside[i] for i in range(4))
        far = tuple(outside[i] for i in range(4))
        depth = jnp.where(at_wall, own[0], far[0])
        norm = jnp.where(at_wall, -own[1], far[1])
        tang = jnp.where(at_wall, own[2], far[2])
        bed = jnp.where(at_wall, own[3], far[3])
        mine = cell_terms(*own[:3])
        other = cell_terms(depth, norm, tang)
        flux = interface(other, mine) if upward else interface(mine, other)
        sign = courant if upward else -courant
        pull = (0.5 * courant * gravity) * own[0] * bed
        return (
            sign * flux[0],
            sign * flux[1] + (pull if upward else -pull),
            sign * flux[2],
        )

    for part, value in enumerate(fluxes(first_ref, top_ref, strip == 0, True)):
        top_sc[part] = value
    for part, value in enumerate(fluxes(last_ref, low_ref, strip == strips - 1, False)):
        low_sc[part] = value
    tiles = out_ref.shape[0]
    tops = out_ref.shape[1]
    out_ref[...] = part_ref[...]
    for tile in range(tiles):
        for part in range(3):
            out_ref[tile, 0, part, 0:1, :] = part_ref[tile, 0, part, 0:1, :] + top_sc[part, tile : tile + 1, :]
            out_ref[tile, tops - 1, part, SUBLANES - 1 : SUBLANES, :] = (
                part_ref[tile, tops - 1, part, SUBLANES - 1 : SUBLANES, :] + low_sc[part, tile : tile + 1, :]
            )


def place_kernel(tiles_ref, out_ref):
    tiles, tops = tiles_ref.shape[:2]
    for tile in range(tiles):
        for top in range(tops):
            for part in range(3):
                out_ref[part, 0, top * SUBLANES : (top + 1) * SUBLANES, tile * LANES : (tile + 1) * LANES] = tiles_ref[
                    tile, top, part
                ]


def whole(count):
    return [pl.BlockSpec(memory_space=pltpu.VMEM)] * count


def params(moved):
    return dict(
        compiler_params=pltpu.CompilerParams(vmem_limit_bytes=16 * 1024 * 1024),
        cost_estimate=pl.CostEstimate(flops=moved * 40, bytes_accessed=moved, transcendentals=0),
    )


def ancestors_of(counts, slot_map):
    total = counts.shape[0]
    places = jnp.arange(total, dtype=jnp.int32)
    upto = (places[None, :] <= places[:, None]).astype(jnp.int32)
    cumul = jnp.sum(upto * counts[None, :], axis=1)
    ordered = jnp.sum((cumul[None, :] <= places[:, None]).astype(jnp.int32), axis=1)
    hits = (slot_map[None, :] == places[:, None]).astype(jnp.int32)
    return jnp.sum(hits * ordered[None, :], axis=1)


def stepped_tiles(state, rain, ground):
    rows, width = ground.shape
    tiles, tops = width // LANES, rows // SUBLANES
    strips = lax.axis_size("row")
    edges = [
        jnp.concatenate([state[:, 0, at], ground[None, at]], axis=0).reshape(4, tiles, LANES) for at in (0, rows - 1)
    ]
    forward = [(i, i + 1) for i in range(strips - 1)]
    backward = [(target, source) for source, target in forward]
    top = lax.ppermute(edges[1], "row", forward)
    low = lax.ppermute(edges[0], "row", backward)
    shape = jax.ShapeDtypeStruct((tiles, tops, 3, SUBLANES, LANES), jnp.float32)
    partial = pl.pallas_call(
        step_kernel, out_shape=shape, in_specs=whole(3), out_specs=whole(1)[0], name="step", **params(2 << 20)
    )(state, rain, ground)
    strip = lax.axis_index("row").astype(jnp.int32).reshape(1)

    return pl.pallas_call(
        functools.partial(edge_kernel, strips=strips),
        out_shape=shape,
        in_specs=[pl.BlockSpec(memory_space=pltpu.SMEM)] + whole(5),
        out_specs=whole(1)[0],
        scratch_shapes=[pltpu.VMEM((3, tiles, LANES), jnp.float32)] * 2,
        input_output_aliases={5: 0},
        name="edges",
        **params(1 << 20),
    )(strip, edges[0], edges[1], top, low, partial)


def placed_strip(block, rows, width):
    return pl.pallas_call(
        place_kernel,
        out_shape=jax.ShapeDtypeStruct((3, 1, rows, width), jnp.float32),
        in_specs=whole(1),
        out_specs=whole(1)[0],
        name="place",
        **params(2 << 20),
    )(block)


def on_device(state, rain, ground, counts, slot_map):
    rows, width = ground.shape
    ancestor = ancestors_of(counts, slot_map)
    block = stepped_tiles(state, rain, ground)
    shape = block.shape
    outgoing = block.reshape((lax.axis_size("dom"), -1) + shape[2:])
    received = lax.all_to_all(outgoing, "dom", split_axis=0, concat_axis=0, tiled=True)
    chosen = jnp.take(received, ancestor, axis=0, mode="clip")
    returned = lax.all_to_all(chosen, "dom", split_axis=0, concat_axis=0, tiled=True)
    return placed_strip(returned.reshape(shape), rows, width)


def solution(mesh):
    placed = (P(None, "dom", "row", None), P("dom", "row", None), P("row", None), P(), P())
    return jax.shard_map(
        on_device,
        mesh=mesh,
        in_specs=placed,
        out_specs=P(None, "dom", "row", None),
        check_vma=False,
    )
```

time: 536 us -> 92.4 us (0.17)
  other arithmetic: 301 us -> 0.34 us
  local copies, waits for them, and re-layouts: 148 us -> 4.56 us
  Pallas kernels: 0 us -> 9.71 us
    unnamed x1 -> x0, other arithmetic: 291 us -> none
    unnamed x15 -> x10, local copies, waits for them, and re-layouts: 78 us -> 1.69 us
    another operation x6 -> x0, local copies, waits for them, and re-layouts: 49.9 us -> none  [the longest x4 48.6 us: advance(): return jnp.stack([new_depth, new_a, new_b])]
    all_to_all x2 -> x0, local copies, waits for them, and re-layouts: 18.1 us -> none  [the longest x1 17.6 us: on_device(): lax.all_to_all(outgoing, 'dom', split_axis=2, concat_axis=0, tiled=True)]
    pallas_call x0 -> x3, Pallas kernels: none -> 9.71 us  [the longest x1 6.56 us: stepped_tiles(): pl.pallas_call(step_kernel, out_shape=shape, in_specs=whole(3), out_specs...]
  transfers between devices with their start and end apart: 3 -> 3, of which waited for: 3 -> 1; matrix products, arithmetic and copies ran while one was open for 0% -> 0% of each run, Pallas kernels for 0% -> 7%
where the time goes in v1:
time: 92.4 us; the launch traced here: 92 us
  blocking collectives  30.5 us (33%)
  waiting for transfers between devices  26.9 us (29%)
  starting transfers between devices  19.9 us (22%)
  Pallas kernels  9.71 us (11%)
  local copies, waits for them, and re-layouts  4.56 us (5%)
    all_to_all x1, blocking collectives, on_device(): lax.all_to_all(chosen, 'dom', split_axis=0, concat_axis=0, tiled=True)  30.5 us
    all_to_all x1, waiting for transfers between devices, on_device(): lax.all_to_all(outgoing, 'dom', split_axis=0, concat_axis=0, tiled=True)  26.9 us
    all_to_all x1, starting transfers between devices, on_device(): lax.all_to_all(outgoing, 'dom', split_axis=0, concat_axis=0, tiled=True)  14.4 us
    pallas_call x1, Pallas kernels, stepped_tiles(): pl.pallas_call(step_kernel, out_shape=shape, in_specs=whole(3), out_specs...  6.56 us
    ppermute x1, starting transfers between devices, stepped_tiles(): top = lax.ppermute(edges[1], 'row', forward)  3.55 us
    pallas_call x1, Pallas kernels, stepped_tiles(): pl.pallas_call(functools.partial(edge_kernel, strips=strips), out_shape=s...  2.22 us
    ppermute x1, starting transfers between devices, stepped_tiles(): low = lax.ppermute(edges[0], 'row', backward)  1.92 us
  transfers between devices with their start and end apart: 3, of which 1 were waited for; matrix products, arithmetic and copies ran while one was open for 0% of the time, Pallas kernels for 7%

profile of v1, /device:TPU:33, one launch (start us, length us, event | category | flops | bytes accessed | tf_op | source)
XLA Modules:
  0.0 92.0 jit_solution(5741662401730983785)
XLA Ops:
  0.0 0.0 copy-start.1
  0.0 0.0 copy-start.2
  0.0 1.2 %fusion = (f32[3,1,1,4096]{3,2,1,0:T(1,128)S(1)}, f32[3,1,1,4096]{3,2,1,0:T(1,128)S(1)}) fusion(f32[3,1,16,4096]{3,2,1,0:T(8,128)} %state_ref.1), kind=kLoop, calls=%fused_computation.10 | loop fusion | bytes 196608 | tf_op jit(solution)/shard_map/slice | solution.py:191
  1.2 1.0 %fusion.1 = (f32[1,4096]{1,0:T(1,128)S(1)}, f32[1,4096]{1,0:T(1,128)S(1)}) fusion(f32[16,4096]{1,0:T(8,128)} %ground_ref.1), kind=kLoop, calls=%fused_computation.11 | loop fusion | bytes 65536 | tf_op jit(solution)/shard_map/slice | solution.py:191
  2.3 3.5 %collective-permute-start = (f32[4,32,128]{2,1,0:T(8,128)S(1)}, f32[4,32,128]{2,1,0:T(8,128)S(1)}, u32[]{:S(2)}, u32[]{:S(2)}) collective-permute-start(f32[4,32,128]{2,1,0:T(8,128)S(1)} %pad_maximum_fusion.1.last_ref), channel_id=1, source_target_pairs={{0,1},{1,2},{2,3},{4,5},{5,6},{6,7},{8,9},{9,10},{10,11},{12,13},{... | collective-permute-start | bytes 196616 | tf_op jit(solution)/shard_map/ppermute | solution.py:195
  5.8 1.9 %collective-permute-start.1 = (f32[4,32,128]{2,1,0:T(8,128)S(1)}, f32[4,32,128]{2,1,0:T(8,128)S(1)}, u32[]{:S(2)}, u32[]{:S(2)}) collective-permute-start(f32[4,32,128]{2,1,0:T(8,128)S(1)} %pad_maximum_fusion.first_ref), channel_id=1, source_target_pairs={{1,0},{2,1},{3,2},{5,4},{6,5},{7,6},{9,8},{10,9},{11,10},{13,12},{... | collective-permute-start | bytes 196616 | tf_op jit(solution)/shard_map/ppermute | solution.py:196
  7.8 0.0 copy-done.1
  7.8 0.0 copy-done.2
  7.8 0.0 copy-start
  7.8 1.1 %copy-done = f32[3,1,16,4096]{3,2,1,0:T(8,128)S(1)} copy-done((f32[3,1,16,4096]{3,2,1,0:T(8,128)S(1)}, f32[3,1,16,4096]{3,2,1,0:T(8,128)}, u32[]{:S(2)}) %copy-start) | copy-done | bytes 786456
  8.9 6.6 %step.1.part_ref = f32[32,2,3,8,128]{4,3,2,1,0:T(8,128)} custom-call(f32[3,1,16,4096]{3,2,1,0:T(8,128)S(1)} %copy-done, f32[1,16,4096]{2,1,0:T(8,128)S(1)} %copy-done.2, f32[16,4096]{1,0:T(8,128)S(1)} %copy-done.1), custom_call_target="tpu_custom_call" | custom-call | flops 83886080 | bytes 2097152 | tf_op jit(solution)/shard_map/step/pallas_call | solution.py:198
  15.5 0.0 collective-permute-done.top_ref
  15.5 0.0 collective-permute-done.1.low_ref
  15.5 2.2 %edges.1 = f32[32,2,3,8,128]{4,3,2,1,0:T(8,128)} custom-call(s32[1]{0:T(128)} %bitcast.strip_ref, f32[4,32,128]{2,1,0:T(8,128)S(1)} %pad_maximum_fusion.first_ref, f32[4,32,128]{2,1,0:T(8,128)S(1)} %pad_maximum_fusion.1.last_ref, f32[4,32,128]{2,1,0:T(8,128)S(1)} %collective-permute-done.top_ref, ...), custom_call_target="tpu_custom_call", output_to_operand_aliasing={{}: (5, {})} | custom-call | flops 41943040 | bytes 1048576 | tf_op jit(solution)/shard_map/edges/pallas_call | solution.py:203
  17.7 0.0 copy-start.3
  17.7 14.4 %all-to-all-start = ((f32[64,1,3,8,128]{4,3,2,1,0:T(8,128)}), f32[64,1,3,8,128]{4,3,2,1,0:T(8,128)S(1)}, u32[]{:S(2)}, u32[]{:S(2)}) async-start(f32[64,1,3,8,128]{4,3,2,1,0:T(8,128)} %bitcast.6), calls=%async_computation | async-start | bytes 1572864 | tf_op jit(solution)/shard_map/all_to_all | solution.py:232
  32.1 0.0 copy-done.3
  32.1 0.1 select_reduce_fusion.1
  32.2 0.0 copy-start.4
  32.2 0.1 convert_reduce_fusion
  32.4 0.5 copy-done.4
  32.9 0.1 select_reduce_fusion
  33.0 26.9 %all-to-all-done = f32[64,1,3,8,128]{4,3,2,1,0:T(8,128)S(1)} async-done(((f32[64,1,3,8,128]{4,3,2,1,0:T(8,128)}), f32[64,1,3,8,128]{4,3,2,1,0:T(8,128)S(1)}, u32[]{:S(2)}, u32[]{:S(2)}) %all-to-all-start) | async-done | bytes 786464 | tf_op jit(solution)/shard_map/all_to_all | solution.py:232
  60.0 0.6 gather_fusion
  60.6 30.5 %all_to_all.10 = f32[64,1,3,8,128]{4,3,2,1,0:T(8,128)S(1)} all-to-all(f32[64,1,3,8,128]{4,3,2,1,0:T(8,128)S(1)} %bitcast.15), channel_id=1, replica_groups=mesh['dom'=64,'row'=4] {'dom'}, dimensions={0} | all-to-all | bytes 1572864 | tf_op jit(solution)/shard_map/all_to_all | solution.py:234
  91.1 0.9 %place.1 = f32[3,1,16,4096]{3,2,1,0:T(8,128)} custom-call(f32[32,2,3,8,128]{4,3,2,1,0:T(8,128)S(1)} %bitcast.13), custom_call_target="tpu_custom_call" | custom-call | flops 83886080 | bytes 2097152 | tf_op jit(solution)/shard_map/place/pallas_call | solution.py:216
  (3 shorter events, 0.0 us)
Async XLA Ops:
  0.0 7.8 %copy-start.1 = (f32[16,4096]{1,0:T(8,128)S(1)}, f32[16,4096]{1,0:T(8,128)}, u32[]{:S(2)}) copy-start(f32[16,4096]{1,0:T(8,128)} %ground_ref.1) | copy-start | bytes 786436
  0.0 7.8 %copy-start.2 = (f32[1,16,4096]{2,1,0:T(8,128)S(1)}, f32[1,16,4096]{2,1,0:T(8,128)}, u32[]{:S(2)}) copy-start(f32[1,16,4096]{2,1,0:T(8,128)} %rain_ref.1) | copy-start | bytes 786436
  2.3 13.2 %collective-permute-start = (f32[4,32,128]{2,1,0:T(8,128)S(1)}, f32[4,32,128]{2,1,0:T(8,128)S(1)}, u32[]{:S(2)}, u32[]{:S(2)}) collective-permute-start(f32[4,32,128]{2,1,0:T(8,128)S(1)} %pad_maximum_fusion.1.last_ref), channel_id=1, source_target_pairs={{0,1},{1,2},{2,3},{4,5},{5,6},{6,7},{8,9},{9,10},{10,11},{12,13},{... | collective-permute-start | bytes 196616 | tf_op jit(solution)/shard_map/ppermute | solution.py:195
  5.8 9.7 %collective-permute-start.1 = (f32[4,32,128]{2,1,0:T(8,128)S(1)}, f32[4,32,128]{2,1,0:T(8,128)S(1)}, u32[]{:S(2)}, u32[]{:S(2)}) collective-permute-start(f32[4,32,128]{2,1,0:T(8,128)S(1)} %pad_maximum_fusion.first_ref), channel_id=1, source_target_pairs={{1,0},{2,1},{3,2},{5,4},{6,5},{7,6},{9,8},{10,9},{11,10},{13,12},{... | collective-permute-start | bytes 196616 | tf_op jit(solution)/shard_map/ppermute | solution.py:196
  7.8 1.1 %copy-start = (f32[3,1,16,4096]{3,2,1,0:T(8,128)S(1)}, f32[3,1,16,4096]{3,2,1,0:T(8,128)}, u32[]{:S(2)}) copy-start(f32[3,1,16,4096]{3,2,1,0:T(8,128)} %state_ref.1) | copy-start | bytes 2359300
  17.7 14.4 %copy-start.3 = (s32[64]{0:T(128)S(1)}, s32[64]{0:T(128)}, u32[]{:S(2)}) copy-start(s32[64]{0:T(128)} %param.8) | copy-start | bytes 772
  17.7 42.2 %all-to-all-start = ((f32[64,1,3,8,128]{4,3,2,1,0:T(8,128)}), f32[64,1,3,8,128]{4,3,2,1,0:T(8,128)S(1)}, u32[]{:S(2)}, u32[]{:S(2)}) async-start(f32[64,1,3,8,128]{4,3,2,1,0:T(8,128)} %bitcast.6), calls=%async_computation | async-start | bytes 1572864 | tf_op jit(solution)/shard_map/all_to_all | solution.py:232
  32.2 0.7 copy-start.4

commit v2 on v1

--- a/solution.py
+++ b/solution.py
@@ -46,7 +46,21 @@
     return by_row, by_col
 
 
-def step_kernel(state_ref, rain_ref, ground_ref, out_ref):
+def pack_kernel(state_ref, ground_ref, first_ref, last_ref, sems):
+    rows = ground_ref.shape[0]
+    copies = []
+    for side, (row, out_ref) in enumerate(((rows - 1, last_ref), (0, first_ref))):
+        at = pl.ds(row, 1)
+        for part in range(3):
+            copies.append(pltpu.make_async_copy(state_ref.at[part, 0, at], out_ref.at[part], sems.at[side, part]))
+        copies.append(pltpu.make_async_copy(ground_ref.at[at], out_ref.at[3], sems.at[side, 3]))
+    for copy in copies:
+        copy.start()
+    for copy in copies:
+        copy.wait()
+
+
+def step_kernel(state_ref, rain_ref, ground_ref, out_ref, *, unroll):
     rows, width = ground_ref.shape
     tiles = width // LANES
     shape = (rows, LANES)
@@ -55,29 +69,34 @@
     first_lane, last_lane = lane == 0, lane == LANES - 1
     first_row, last_row = row == 0, row == rows - 1
 
+    def columns(tile):
+        start = tile * LANES
+        return pl.ds(start if isinstance(tile, int) else pl.multiple_of(start, LANES), LANES)
+
     def load(tile):
-        at = pl.ds(pl.multiple_of(tile * LANES, LANES), LANES)
+        at = columns(tile)
         return state_ref[0, 0, :, at], state_ref[1, 0, :, at], state_ref[2, 0, :, at], ground_ref[:, at]
 
     def rolled(terms):
         return tuple(pltpu.roll(term, LANES - 1, 1) for term in terms)
 
-    def one(tile, carry):
-        cells, bed, cells_r, bed_r, flux_before, bed_before = carry
-        depth, flow_a, flow_b = cells[0]
-        by_row, by_col = cells[1], cells[2]
-        nxt = jnp.minimum(tile + 1, tiles - 1)
-        n_depth, n_a, n_b, n_bed = load(nxt)
-        n_row, n_col = both_ways(n_depth, n_a, n_b)
-        n_rolled = rolled(n_col)
-        n_bed_r = pltpu.roll(n_bed, LANES - 1, 1)
+    def mirrored(terms):
+        depth, norm, tang, fnorm, ftang, slow, fast = terms
+        return depth, -norm, tang, fnorm, -ftang, -fast, -slow
+
+    def one(tile, carry, last=False):
+        by_row, by_col, bed, cells_r, bed_r, flux_before, bed_before = carry
+        depth, flow_a, flow_b = by_row[:3]
+        if last:
+            n_row, n_col, n_bed = by_row, by_col, bed
+            n_rolled, n_bed_r = mirrored(by_col), bed
+        else:
+            n_depth, n_a, n_b, n_bed = load(tile + 1)
+            n_row, n_col = both_ways(n_depth, n_a, n_b)
+            n_rolled = rolled(n_col)
+            n_bed_r = pltpu.roll(n_bed, LANES - 1, 1)
         right = tuple(jnp.where(last_lane, n, c) for n, c in zip(n_rolled, cells_r))
-        at_wall = tile == tiles - 1
-        ghost = jnp.logical_and(last_lane, at_wall)
-        g_depth, g_norm, g_tang, g_fnorm, g_ftang, g_slow, g_fast = by_col
-        mirror = (g_depth, -g_norm, g_tang, g_fnorm, -g_ftang, -g_fast, -g_slow)
-        right = tuple(jnp.where(ghost, m, r) for m, r in zip(mirror, right))
-        bed_next = jnp.where(ghost, bed, jnp.where(last_lane, n_bed_r, bed_r))
+        bed_next = jnp.where(last_lane, n_bed_r, bed_r)
         flux = interface(by_col, right)
         flux_r = tuple(pltpu.roll(f, 1, 1) for f in flux)
         flux_left = tuple(jnp.where(first_lane, b, f) for b, f in zip(flux_before, flux_r))
@@ -92,28 +111,28 @@
         bed_down = jnp.where(last_row, 0.0, pltpu.roll(bed, rows - 1, 0))
 
         pull = (0.5 * courant * gravity) * depth
-        at = pl.ds(pl.multiple_of(tile * LANES, LANES), LANES)
-        new_depth = depth - courant * ((below[0] - inner[0]) + (flux[0] - flux_left[0])) + rain_ref[0, :, at]
+        new_depth = depth - courant * ((below[0] - inner[0]) + (flux[0] - flux_left[0])) + rain_ref[0, :, columns(tile)]
         new_a = flow_a - courant * ((below[1] - inner[1]) + (flux[2] - flux_left[2])) - pull * (bed_down - bed_up)
         new_b = flow_b - courant * ((below[2] - inner[2]) + (flux[1] - flux_left[1])) - pull * (bed_next - bed_left)
         for part, value in enumerate((new_depth, new_a, new_b)):
             for top in range(rows // SUBLANES):
                 out_ref[tile, top, part] = value[top * SUBLANES : (top + 1) * SUBLANES]
-        return ((n_depth, n_a, n_b), n_row, n_col), n_bed, n_rolled, n_bed_r, flux_r, bed_rolled
+        return n_row, n_col, n_bed, n_rolled, n_bed_r, flux_r, bed_rolled
 
     depth, flow_a, flow_b, bed = load(0)
     by_row, by_col = both_ways(depth, flow_a, flow_b)
-    g_depth, g_norm, g_tang, g_fnorm, g_ftang, g_slow, g_fast = by_col
-    mirror = (g_depth, -g_norm, g_tang, g_fnorm, -g_ftang, -g_fast, -g_slow)
-    start = (
-        ((depth, flow_a, flow_b), by_row, by_col),
-        bed,
-        rolled(by_col),
-        pltpu.roll(bed, LANES - 1, 1),
-        interface(mirror, by_col),
-        bed,
-    )
-    lax.fori_loop(0, tiles, one, start)
+    edge = interface(mirrored(by_col), by_col)
+    carry = (by_row, by_col, bed, rolled(by_col), pltpu.roll(bed, LANES - 1, 1), edge, bed)
+    steps = (tiles - 1) // unroll
+
+    def some(i, carry):
+        for k in range(unroll):
+            carry = one(i * unroll + k, carry)
+        return carry
+
+    carry = lax.fori_loop(0, steps, some, carry)
+    for tile in range(steps * unroll, tiles):
+        carry = one(tile, carry, tile == tiles - 1)
 
 
 def edge_kernel(strip_ref, first_ref, last_ref, top_ref, low_ref, part_ref, out_ref, top_sc, low_sc, *, strips):
@@ -152,6 +171,11 @@
             )
 
 
+def choose_kernel(index_ref, from_ref, out_ref):
+    for slot in range(out_ref.shape[0]):
+        out_ref[slot] = from_ref[index_ref[slot]]
+
+
 def place_kernel(tiles_ref, out_ref):
     tiles, tops = tiles_ref.shape[:2]
     for tile in range(tiles):
@@ -183,33 +207,69 @@
     return jnp.sum(hits * ordered[None, :], axis=1)
 
 
+UNROLL = 4
+HBM = pl.BlockSpec(memory_space=pltpu.HBM)
+
+
+def packed_edges(state, ground):
+    rows, width = ground.shape
+    shape = pltpu.VMEM((4, 1, width), jnp.float32)
+    return pl.pallas_call(
+        pack_kernel,
+        out_shape=(shape, shape),
+        in_specs=[HBM, HBM],
+        out_specs=whole(2),
+        scratch_shapes=[pltpu.SemaphoreType.DMA((2, 4))],
+        name="pack",
+        **params(1 << 18),
+    )(*(pltpu.with_memory_space_constraint(x, pltpu.HBM) for x in (state, ground)))
+
+
+def partial_step(state, rain, ground, unroll=UNROLL):
+    rows, width = ground.shape
+    tiles, tops = width // LANES, rows // SUBLANES
+    return pl.pallas_call(
+        functools.partial(step_kernel, unroll=unroll),
+        out_shape=pltpu.VMEM((tiles, tops, 3, SUBLANES, LANES), jnp.float32),
+        in_specs=whole(3),
+        out_specs=whole(1)[0],
+        name="step",
+        **params(8 << 20),
+    )(state, rain, ground)
+
+
 def stepped_tiles(state, rain, ground):
     rows, width = ground.shape
-    tiles, tops = width // LANES, rows // SUBLANES
+    tiles = width // LANES
     strips = lax.axis_size("row")
-    edges = [
-        jnp.concatenate([state[:, 0, at], ground[None, at]], axis=0).reshape(4, tiles, LANES) for at in (0, rows - 1)
-    ]
+    first, last = packed_edges(state, ground)
     forward = [(i, i + 1) for i in range(strips - 1)]
     backward = [(target, source) for source, target in forward]
-    top = lax.ppermute(edges[1], "row", forward)
-    low = lax.ppermute(edges[0], "row", backward)
-    shape = jax.ShapeDtypeStruct((tiles, tops, 3, SUBLANES, LANES), jnp.float32)
-    partial = pl.pallas_call(
-        step_kernel, out_shape=shape, in_specs=whole(3), out_specs=whole(1)[0], name="step", **params(2 << 20)
-    )(state, rain, ground)
+    top = lax.ppermute(last, "row", forward)
+    low = lax.ppermute(first, "row", backward)
+    partial = partial_step(state, rain, ground)
     strip = lax.axis_index("row").astype(jnp.int32).reshape(1)
-
+    square = (4, tiles, LANES)
     return pl.pallas_call(
         functools.partial(edge_kernel, strips=strips),
-        out_shape=shape,
+        out_shape=pltpu.VMEM(partial.shape, jnp.float32),
         in_specs=[pl.BlockSpec(memory_space=pltpu.SMEM)] + whole(5),
         out_specs=whole(1)[0],
         scratch_shapes=[pltpu.VMEM((3, tiles, LANES), jnp.float32)] * 2,
-        input_output_aliases={5: 0},
         name="edges",
         **params(1 << 20),
-    )(strip, edges[0], edges[1], top, low, partial)
+    )(strip, first.reshape(square), last.reshape(square), top.reshape(square), low.reshape(square), partial)
+
+
+def chosen_blocks(index, blocks):
+    return pl.pallas_call(
+        choose_kernel,
+        out_shape=jax.ShapeDtypeStruct(index.shape + blocks.shape[1:], jnp.float32),
+        in_specs=[pl.BlockSpec(memory_space=pltpu.SMEM)] + whole(1),
+        out_specs=whole(1)[0],
+        name="choose",
+        **params(2 << 20),
+    )(index, blocks)
 
 
 def placed_strip(block, rows, width):
@@ -226,11 +286,11 @@
 def on_device(state, rain, ground, counts, slot_map):
     rows, width = ground.shape
     ancestor = ancestors_of(counts, slot_map)
-    block = stepped_tiles(state, rain, ground)
+    block, ancestor = lax.optimization_barrier((stepped_tiles(state, rain, ground), ancestor))
     shape = block.shape
     outgoing = block.reshape((lax.axis_size("dom"), -1) + shape[2:])
     received = lax.all_to_all(outgoing, "dom", split_axis=0, concat_axis=0, tiled=True)
-    chosen = jnp.take(received, ancestor, axis=0, mode="clip")
+    chosen = chosen_blocks(ancestor, received)
     returned = lax.all_to_all(chosen, "dom", split_axis=0, concat_axis=0, tiled=True)
     return placed_strip(returned.reshape(shape), rows, width)
 

time: 92.4 us -> 84.7 us (0.917)
  blocking collectives: 30.5 us -> 72.4 us
  waiting for transfers between devices: 26.9 us -> 0.01 us
  starting transfers between devices: 19.9 us -> 5.47 us
  Pallas kernels: 9.71 us -> 4.66 us
  local copies, waits for them, and re-layouts: 4.56 us -> 1.51 us
    all_to_all x0 -> x1, blocking collectives: none -> 41.9 us  [on_device(): lax.all_to_all(outgoing, 'dom', split_axis=0, concat_axis=0, tiled=True)]
    all_to_all x1 -> x0, waiting for transfers between devices: 26.9 us -> none  [on_device(): lax.all_to_all(outgoing, 'dom', split_axis=0, concat_axis=0, tiled=True)]
    all_to_all x1 -> x0, starting transfers between devices: 14.4 us -> none  [on_device(): lax.all_to_all(outgoing, 'dom', split_axis=0, concat_axis=0, tiled=True)]
    pallas_call x2 -> x4, Pallas kernels: 8.78 us -> 3.73 us  [the longest x1 1.94 us: partial_step(): pl.pallas_call(functools.partial(step_kernel, unroll=unroll), out_shape=p...]
    slice x2 -> x0, local copies, waits for them, and re-layouts: 2.24 us -> none  [the longest x1 1.24 us: stepped_tiles(): state[:, 0, at]]
  transfers between devices with their start and end apart: 3 -> 2, of which waited for: 1 -> 0; matrix products, arithmetic and copies ran while one was open for 0% -> 0% of each run, Pallas kernels for 7% -> 2%
where the time goes in v2:
time: 84.7 us; the launch traced here: 84.5 us
  blocking collectives  72.4 us (85%)
  starting transfers between devices  5.47 us (6%)
  Pallas kernels  4.66 us (6%)
  local copies, waits for them, and re-layouts  1.51 us (2%)
    all_to_all x1, blocking collectives, on_device(): lax.all_to_all(outgoing, 'dom', split_axis=0, concat_axis=0, tiled=True)  41.9 us
    all_to_all x1, blocking collectives, on_device(): lax.all_to_all(chosen, 'dom', split_axis=0, concat_axis=0, tiled=True)  30.5 us
    ppermute x1, starting transfers between devices, stepped_tiles(): top = lax.ppermute(last, 'row', forward)  3.55 us
    pallas_call x1, Pallas kernels, partial_step(): pl.pallas_call(functools.partial(step_kernel, unroll=unroll), out_shape=p...  1.94 us
    ppermute x1, starting transfers between devices, stepped_tiles(): low = lax.ppermute(first, 'row', backward)  1.92 us
  transfers between devices with their start and end apart: 2, of which 0 were waited for; matrix products, arithmetic and copies ran while one was open for 0% of the time, Pallas kernels for 2%

profile of v2, /device:TPU:33, one launch (start us, length us, event | category | flops | bytes accessed | tf_op | source)
XLA Modules:
  0.0 84.5 jit_solution(11401222960972666138)
XLA Ops:
  0.0 0.0 copy-start
  0.0 0.0 copy-start.1
  0.0 1.0 %pack.1 = (f32[4,1,4096]{2,1,0:T(1,128)S(1)}, f32[4,1,4096]{2,1,0:T(1,128)S(1)}) custom-call(f32[3,1,16,4096]{3,2,1,0:T(8,128)} %state_ref.3, f32[16,4096]{1,0:T(8,128)} %ground_ref.3), custom_call_target="tpu_custom_call" | custom-call | flops 10485760 | bytes 262144 | tf_op jit(solution)/shard_map/pack/pallas_call | solution.py:217
  1.0 0.0 copy-start.3
  1.0 3.5 %collective-permute-start = (f32[4,1,4096]{2,1,0:T(1,128)S(1)}, f32[4,1,4096]{2,1,0:T(1,128)S(1)}, u32[]{:S(2)}, u32[]{:S(2)}) collective-permute-start(f32[4,1,4096]{2,1,0:T(1,128)S(1)} %get-tuple-element.10), channel_id=1, source_target_pairs={{0,1},{1,2},{2,3},{4,5},{5,6},{6,7},{8,9},{9,10},{10,11},{12,13},{... | collective-permute-start | bytes 196616 | tf_op jit(solution)/shard_map/ppermute | solution.py:248
  4.6 1.9 %collective-permute-start.1 = (f32[4,1,4096]{2,1,0:T(1,128)S(1)}, f32[4,1,4096]{2,1,0:T(1,128)S(1)}, u32[]{:S(2)}, u32[]{:S(2)}) collective-permute-start(f32[4,1,4096]{2,1,0:T(1,128)S(1)} %get-tuple-element.9), channel_id=1, source_target_pairs={{1,0},{2,1},{3,2},{5,4},{6,5},{7,6},{9,8},{10,9},{11,10},{13,12},{... | collective-permute-start | bytes 196616 | tf_op jit(solution)/shard_map/ppermute | solution.py:249
  6.5 0.0 copy-done.3
  6.5 0.1 select_reduce_fusion.1
  6.6 0.0 copy-start.4
  6.6 0.1 convert_reduce_fusion
  6.7 0.5 copy-done.4
  7.3 0.1 select_reduce_fusion.index_ref
  7.4 0.0 copy-done
  7.4 0.0 copy-done.1
  7.4 0.0 copy-start.2
  7.4 0.9 %copy-done.2 = f32[1,16,4096]{2,1,0:T(8,128)S(1)} copy-done((f32[1,16,4096]{2,1,0:T(8,128)S(1)}, f32[1,16,4096]{2,1,0:T(8,128)}, u32[]{:S(2)}) %copy-start.2) | copy-done | bytes 262168
  8.4 1.9 %step.1.part_ref = f32[32,2,3,8,128]{4,3,2,1,0:T(8,128)S(1)} custom-call(f32[3,1,16,4096]{3,2,1,0:T(8,128)S(1)} %copy-done, f32[1,16,4096]{2,1,0:T(8,128)S(1)} %copy-done.2, f32[16,4096]{1,0:T(8,128)S(1)} %copy-done.1), custom_call_target="tpu_custom_call" | custom-call | flops 335544320 | bytes 8388608 | tf_op jit(solution)/shard_map/step/pallas_call | solution.py:231
  10.3 0.0 collective-permute-done
  10.3 0.0 collective-permute-done.1
  10.3 0.2 edges.1
  10.5 41.9 %all_to_all.10.from_ref = f32[64,1,3,8,128]{4,3,2,1,0:T(8,128)S(1)} all-to-all(f32[64,1,3,8,128]{4,3,2,1,0:T(8,128)S(1)} %bitcast.7), channel_id=1, replica_groups=mesh['dom'=64,'row'=4] {'dom'}, dimensions={0} | all-to-all | bytes 1572864 | tf_op jit(solution)/shard_map/all_to_all | solution.py:292
  52.5 0.6 choose.1
  53.1 30.5 %all_to_all.11 = f32[64,1,3,8,128]{4,3,2,1,0:T(8,128)S(1)} all-to-all(f32[64,1,3,8,128]{4,3,2,1,0:T(8,128)S(1)} %choose.1), channel_id=1, replica_groups=mesh['dom'=64,'row'=4] {'dom'}, dimensions={0} | all-to-all | bytes 1572864 | tf_op jit(solution)/shard_map/all_to_all | solution.py:294
  83.6 0.9 %place.1 = f32[3,1,16,4096]{3,2,1,0:T(8,128)} custom-call(f32[32,2,3,8,128]{4,3,2,1,0:T(8,128)S(1)} %bitcast.8), custom_call_target="tpu_custom_call" | custom-call | flops 83886080 | bytes 2097152 | tf_op jit(solution)/shard_map/place/pallas_call | solution.py:276
Async XLA Ops:
  0.0 7.4 %copy-start = (f32[3,1,16,4096]{3,2,1,0:T(8,128)S(1)}, f32[3,1,16,4096]{3,2,1,0:T(8,128)}, u32[]{:S(2)}) copy-start(f32[3,1,16,4096]{3,2,1,0:T(8,128)} %state_ref.3) | copy-start | bytes 2359300
  0.0 7.4 %copy-start.1 = (f32[16,4096]{1,0:T(8,128)S(1)}, f32[16,4096]{1,0:T(8,128)}, u32[]{:S(2)}) copy-start(f32[16,4096]{1,0:T(8,128)} %ground_ref.3) | copy-start | bytes 786436
  1.0 5.5 %copy-start.3 = (s32[64]{0:T(128)S(1)}, s32[64]{0:T(128)}, u32[]{:S(2)}) copy-start(s32[64]{0:T(128)} %param.8) | copy-start | bytes 772
  1.0 9.3 %collective-permute-start = (f32[4,1,4096]{2,1,0:T(1,128)S(1)}, f32[4,1,4096]{2,1,0:T(1,128)S(1)}, u32[]{:S(2)}, u32[]{:S(2)}) collective-permute-start(f32[4,1,4096]{2,1,0:T(1,128)S(1)} %get-tuple-element.10), channel_id=1, source_target_pairs={{0,1},{1,2},{2,3},{4,5},{5,6},{6,7},{8,9},{9,10},{10,11},{12,13},{... | collective-permute-start | bytes 196616 | tf_op jit(solution)/shard_map/ppermute | solution.py:248
  4.6 5.8 %collective-permute-start.1 = (f32[4,1,4096]{2,1,0:T(1,128)S(1)}, f32[4,1,4096]{2,1,0:T(1,128)S(1)}, u32[]{:S(2)}, u32[]{:S(2)}) collective-permute-start(f32[4,1,4096]{2,1,0:T(1,128)S(1)} %get-tuple-element.9), channel_id=1, source_target_pairs={{1,0},{2,1},{3,2},{5,4},{6,5},{7,6},{9,8},{10,9},{11,10},{13,12},{... | collective-permute-start | bytes 196616 | tf_op jit(solution)/shard_map/ppermute | solution.py:249
  6.6 0.7 copy-start.4
  7.4 1.0 %copy-start.2 = (f32[1,16,4096]{2,1,0:T(8,128)S(1)}, f32[1,16,4096]{2,1,0:T(8,128)}, u32[]{:S(2)}) copy-start(f32[1,16,4096]{2,1,0:T(8,128)} %rain_ref.1) | copy-start | bytes 786436

commit v3 on v2

--- a/solution.py
+++ b/solution.py
@@ -171,9 +171,77 @@
             )
 
 
-def choose_kernel(index_ref, from_ref, out_ref):
+def plan_kernel(zh_ref, core_ref, counts_ref, slot_ref, plan_ref, level_ref, *, sizes):
+    zh, core = zh_ref[0], core_ref[0]
+    total = counts_ref.shape[1]
+    square = (total, total)
+    i = lax.broadcasted_iota(jnp.int32, square, 0)
+    j = lax.broadcasted_iota(jnp.int32, square, 1)
+
+    def over_lanes(values):
+        return jnp.sum(values, axis=1, keepdims=True)
+
+    def over_rows(values):
+        return jnp.sum(values, axis=0, keepdims=True)
+
+    def half(places):
+        return jnp.bitwise_and(jnp.right_shift(places, 1), 1)
+
+    counts, slots = counts_ref[...], slot_ref[...]
+    cumul = over_lanes(jnp.where(j <= i, counts, 0))
+    ordered = over_rows((cumul <= j).astype(jnp.int32))
+    ancestor = over_lanes(jnp.where(slots == i, ordered, 0))
+    crossing = jnp.logical_and(ancestor == j, half(i) != half(j))
+    needed = (over_rows(crossing.astype(jnp.int32)) > 0).astype(jnp.int32)
+    needed_col = over_lanes(jnp.where(i == j, needed, 0))
+    earlier = jnp.logical_and(i < j, half(i) == half(j))
+    rank = over_rows(jnp.where(earlier, needed_col, 0))
+    rank_col = over_lanes(jnp.where(i == j, rank, 0))
+    home = jnp.where(jnp.bitwise_and(i, 1) == core, 0, total) + jnp.right_shift(i, 2)
+    mine = jnp.logical_and(half(i) == zh, jnp.logical_and(needed_col > 0, rank_col == j))
+    send = over_rows(jnp.where(mine, home, 0))
+    rank_of = over_lanes(jnp.where(ancestor == j, rank, 0))
+    here = jnp.where(jnp.bitwise_and(ancestor, 1) == core, 0, total) + jnp.right_shift(ancestor, 2)
+    source = jnp.where(half(ancestor) == zh, here, 2 * total + rank_of)
+    find = over_rows(jnp.where(i == 4 * j + 2 * zh + core, source, 0))
+    plan_ref[0:1, :] = send
+    plan_ref[1:2, :] = find
+    lower = jnp.sum(jnp.where(half(j[0:1]) == 0, needed, 0))
+    most = jnp.maximum(lower, jnp.sum(needed) - lower)
+    level_ref[0] = sum((most > size).astype(jnp.int32) for size in sizes[:-1])
+
+
+def outgoing_kernel(core_ref, plan_ref, own_ref, other_ref, out_ref):
+    core = core_ref[0]
+    for k in range(out_ref.shape[0]):
+        code = plan_ref[0, k]
+
+        @pl.when(code < 64)
+        def _():
+            out_ref[k] = own_ref[code, core]
+
+        @pl.when(code >= 64)
+        def _():
+            out_ref[k] = other_ref[code - 64, core]
+
+
+def slots_kernel(core_ref, plan_ref, own_ref, other_ref, crossed_ref, crossed_other_ref, out_ref):
+    core = core_ref[0]
     for slot in range(out_ref.shape[0]):
-        out_ref[slot] = from_ref[index_ref[slot]]
+        code = plan_ref[1, slot]
+
+        @pl.when(code < 64)
+        def _():
+            out_ref[slot] = own_ref[code]
+
+        @pl.when(jnp.logical_and(code >= 64, code < 128))
+        def _():
+            out_ref[slot] = other_ref[code - 64]
+
+        @pl.when(code >= 128)
+        def _():
+            out_ref[slot, core] = crossed_ref[code - 128]
+            out_ref[slot, 1 - core] = crossed_other_ref[code - 128]
 
 
 def place_kernel(tiles_ref, out_ref):
@@ -195,16 +263,6 @@
         compiler_params=pltpu.CompilerParams(vmem_limit_bytes=16 * 1024 * 1024),
         cost_estimate=pl.CostEstimate(flops=moved * 40, bytes_accessed=moved, transcendentals=0),
     )
-
-
-def ancestors_of(counts, slot_map):
-    total = counts.shape[0]
-    places = jnp.arange(total, dtype=jnp.int32)
-    upto = (places[None, :] <= places[:, None]).astype(jnp.int32)
-    cumul = jnp.sum(upto * counts[None, :], axis=1)
-    ordered = jnp.sum((cumul[None, :] <= places[:, None]).astype(jnp.int32), axis=1)
-    hits = (slot_map[None, :] == places[:, None]).astype(jnp.int32)
-    return jnp.sum(hits * ordered[None, :], axis=1)
 
 
 UNROLL = 4
@@ -261,15 +319,41 @@
     )(strip, first.reshape(square), last.reshape(square), top.reshape(square), low.reshape(square), partial)
 
 
-def chosen_blocks(index, blocks):
-    return pl.pallas_call(
-        choose_kernel,
-        out_shape=jax.ShapeDtypeStruct(index.shape + blocks.shape[1:], jnp.float32),
-        in_specs=[pl.BlockSpec(memory_space=pltpu.SMEM)] + whole(1),
+SMEM = pl.BlockSpec(memory_space=pltpu.SMEM)
+SWAP = [(0, 1), (1, 0)]
+
+
+def transfer_plan(zh, core, counts, slot_map):
+    total = counts.shape[0]
+    return pl.pallas_call(
+        functools.partial(plan_kernel, sizes=SIZES),
+        out_shape=(jax.ShapeDtypeStruct((2, total), jnp.int32), jax.ShapeDtypeStruct((1,), jnp.int32)),
+        in_specs=[SMEM, SMEM] + whole(2),
+        out_specs=(whole(1)[0], SMEM),
+        name="plan",
+        **params(1 << 16),
+    )(zh, core, counts.reshape(1, total), slot_map.reshape(1, total))
+
+
+def blocks_for_slots(core, plan, own, other, most):
+    outgoing = pl.pallas_call(
+        outgoing_kernel,
+        out_shape=jax.ShapeDtypeStruct((most,) + own.shape[2:], jnp.float32),
+        in_specs=[SMEM, SMEM] + whole(2),
         out_specs=whole(1)[0],
-        name="choose",
+        name="outgoing",
+        **params(1 << 20),
+    )(core, plan, own, other)
+    crossed = lax.ppermute(outgoing, "zh", SWAP)
+    crossed_other = lax.ppermute(crossed, "core", SWAP)
+    return pl.pallas_call(
+        slots_kernel,
+        out_shape=jax.ShapeDtypeStruct(own.shape, jnp.float32),
+        in_specs=[SMEM, SMEM] + whole(4),
+        out_specs=whole(1)[0],
+        name="slots",
         **params(2 << 20),
-    )(index, blocks)
+    )(core, plan, own, other, crossed, crossed_other)
 
 
 def placed_strip(block, rows, width):
@@ -283,24 +367,36 @@
     )(block)
 
 
+PLANE = ("y", "x")
+SIZES = (8, 10, 12, 14, 16, 18, 20, 24, 32)
+
+
 def on_device(state, rain, ground, counts, slot_map):
     rows, width = ground.shape
-    ancestor = ancestors_of(counts, slot_map)
-    block, ancestor = lax.optimization_barrier((stepped_tiles(state, rain, ground), ancestor))
+    zh = lax.axis_index("zh").astype(jnp.int32).reshape(1)
+    core = lax.axis_index("core").astype(jnp.int32).reshape(1)
+    plan, level = transfer_plan(zh, core, counts, slot_map)
+    block, plan, level = lax.optimization_barrier((stepped_tiles(state, rain, ground), plan, level))
     shape = block.shape
-    outgoing = block.reshape((lax.axis_size("dom"), -1) + shape[2:])
-    received = lax.all_to_all(outgoing, "dom", split_axis=0, concat_axis=0, tiled=True)
-    chosen = chosen_blocks(ancestor, received)
-    returned = lax.all_to_all(chosen, "dom", split_axis=0, concat_axis=0, tiled=True)
+    spread = lax.axis_size("y") * lax.axis_size("x")
+    outgoing = block.reshape((spread, 2, -1) + shape[2:])
+    own = lax.all_to_all(outgoing, PLANE, split_axis=0, concat_axis=0, tiled=True)
+    other = lax.ppermute(own, "core", SWAP)
+    chosen = lax.switch(
+        level[0], [functools.partial(blocks_for_slots, most=size) for size in SIZES], core, plan, own, other
+    )
+    returned = lax.all_to_all(chosen, PLANE, split_axis=0, concat_axis=0, tiled=True)
     return placed_strip(returned.reshape(shape), rows, width)
 
 
 def solution(mesh):
-    placed = (P(None, "dom", "row", None), P("dom", "row", None), P("row", None), P(), P())
+    fine = Mesh(mesh.devices.reshape(4, 4, 2, 2, 4), ("y", "x", "zh", "core", "row"))
+    dom = ("y", "x", "zh", "core")
+    placed = (P(None, dom, "row", None), P(dom, "row", None), P("row", None), P(), P())
     return jax.shard_map(
         on_device,
-        mesh=mesh,
+        mesh=fine,
         in_specs=placed,
-        out_specs=P(None, "dom", "row", None),
+        out_specs=P(None, dom, "row", None),
         check_vma=False,
     )

time: 84.7 us -> 77.6 us (0.916)
  the two profiles are of different devices: /device:TPU:33 before, /device:TPU:32 now
where the time goes in v3:
time: 77.6 us; the launch traced here: 78.5 us
  blocking collectives  38.4 us (49%)
  waiting for transfers between devices  18.8 us (24%)
  starting transfers between devices  12.1 us (16%)
  Pallas kernels  6.57 us (8%)
  local copies, waits for them, and re-layouts  1.61 us (2%)
    all_to_all x1, blocking collectives, on_device(): lax.all_to_all(outgoing, PLANE, split_axis=0, concat_axis=0, tiled=True)  20.8 us
    all_to_all x1, blocking collectives, on_device(): lax.all_to_all(chosen, PLANE, split_axis=0, concat_axis=0, tiled=True)  17.6 us
    ppermute x1, waiting for transfers between devices, blocks_for_slots(): crossed = lax.ppermute(outgoing, 'zh', SWAP)  15.6 us
    ppermute x1, starting transfers between devices, blocks_for_slots(): crossed = lax.ppermute(outgoing, 'zh', SWAP)  6.19 us
    ppermute x1, starting transfers between devices, stepped_tiles(): low = lax.ppermute(first, 'row', backward)  3.75 us
    ppermute x1, starting transfers between devices, stepped_tiles(): top = lax.ppermute(last, 'row', forward)  2.09 us
    pallas_call x1, Pallas kernels, partial_step(): pl.pallas_call(functools.partial(step_kernel, unroll=unroll), out_shape=p...  1.94 us
    ppermute x1, waiting for transfers between devices, on_device(): other = lax.ppermute(own, 'core', SWAP)  1.66 us
  transfers between devices with their start and end apart: 5, of which 3 were waited for; matrix products, arithmetic and copies ran while one was open for 0% of the time, Pallas kernels for 4%

profile of v3, /device:TPU:32, one launch (start us, length us, event | category | flops | bytes accessed | tf_op | source)
XLA Modules:
  0.0 78.5 jit_solution(7607791811608973237)
XLA Ops:
  0.0 0.0 copy-start.1
  0.0 0.0 copy-start
  0.0 1.0 %pack.1 = (f32[4,1,4096]{2,1,0:T(1,128)S(1)}, f32[4,1,4096]{2,1,0:T(1,128)S(1)}) custom-call(f32[3,1,16,4096]{3,2,1,0:T(8,128)} %state_ref.3, f32[16,4096]{1,0:T(8,128)} %ground_ref.3), custom_call_target="tpu_custom_call" | custom-call | flops 10485760 | bytes 262144 | tf_op jit(solution)/shard_map/pack/pallas_call | solution.py:275
  1.0 3.8 %collective-permute-start.19 = (f32[4,1,4096]{2,1,0:T(1,128)S(1)}, f32[4,1,4096]{2,1,0:T(1,128)S(1)}, u32[]{:S(2)}, u32[]{:S(2)}) collective-permute-start(f32[4,1,4096]{2,1,0:T(1,128)S(1)} %get-tuple-element.130), channel_id=1, source_target_pairs={{1,0},{2,1},{3,2},{5,4},{6,5},{7,6},{9,8},{10,9},{11,10},{13,12},{... | collective-permute-start | bytes 196616 | tf_op jit(solution)/shard_map/ppermute | solution.py:307
  4.7 2.1 %collective-permute-start.18 = (f32[4,1,4096]{2,1,0:T(1,128)S(1)}, f32[4,1,4096]{2,1,0:T(1,128)S(1)}, u32[]{:S(2)}, u32[]{:S(2)}) collective-permute-start(f32[4,1,4096]{2,1,0:T(1,128)S(1)} %get-tuple-element.131), channel_id=1, source_target_pairs={{0,1},{1,2},{2,3},{4,5},{5,6},{6,7},{8,9},{9,10},{10,11},{12,13},{... | collective-permute-start | bytes 196616 | tf_op jit(solution)/shard_map/ppermute | solution.py:306
  6.9 0.0 copy-start.3
  6.9 0.0 copy-start.4
  6.9 0.6 copy-done.3
  7.5 0.0 copy-done.4
  7.5 0.9 %plan.1 = (s32[2,64]{1,0:T(2,128)S(1)}, s32[1]{0:T(128)}) custom-call(s32[1]{0:T(128)} %bitcast.5.zh_ref, s32[1]{0:T(128)} %bitcast.6.core_ref, s32[1,64]{1,0:T(1,128)S(1)} %bitcast.18, s32[1,64]{1,0:T(1,128)S(1)} %bitcast.19), custom_call_target="tpu_custom_call" | custom-call | flops 2621440 | bytes 65536 | tf_op jit(solution)/shard_map/plan/pallas_call | solution.py:328
  8.4 0.0 copy-done.1
  8.4 0.0 copy-done
  8.4 0.0 copy-start.2
  8.4 0.9 %copy-done.2 = f32[1,16,4096]{2,1,0:T(8,128)S(1)} copy-done((f32[1,16,4096]{2,1,0:T(8,128)S(1)}, f32[1,16,4096]{2,1,0:T(8,128)}, u32[]{:S(2)}) %copy-start.2) | copy-done | bytes 262168
  9.4 1.9 %step.1.part_ref = f32[32,2,3,8,128]{4,3,2,1,0:T(8,128)S(1)} custom-call(f32[3,1,16,4096]{3,2,1,0:T(8,128)S(1)} %copy-done, f32[1,16,4096]{2,1,0:T(8,128)S(1)} %copy-done.2, f32[16,4096]{1,0:T(8,128)S(1)} %copy-done.1), custom_call_target="tpu_custom_call" | custom-call | flops 335544320 | bytes 8388608 | tf_op jit(solution)/shard_map/step/pallas_call | solution.py:289
  11.3 0.0 collective-permute-done.19
  11.3 0.0 collective-permute-done.18
  11.4 0.2 edges.1
  11.6 20.8 %all_to_all.10 = f32[16,2,2,3,8,128]{5,4,3,2,1,0:T(8,128)S(1)} all-to-all(f32[16,2,2,3,8,128]{5,4,3,2,1,0:T(8,128)S(1)} %bitcast.12), channel_id=1, replica_groups=mesh['y'=4,'x'=4,'zh'=2,'core'=2,'row'=4] {'y','x'}, dimensions={0} | all-to-all | bytes 1572864 | tf_op jit(solution)/shard_map/all_to_all | solution.py:383
  32.4 0.0 collective-permute-start.20
  33.0 1.7 %collective-permute-done.20 = f32[16,2,2,3,8,128]{5,4,3,2,1,0:T(8,128)S(1)} collective-permute-done((f32[16,2,2,3,8,128]{5,4,3,2,1,0:T(8,128)S(1)}, f32[16,2,2,3,8,128]{5,4,3,2,1,0:T(8,128)S(1)}, u32[]{:S(2)}, u32[]{:S(2)}) %collective-permute-start.20) | collective-permute-done | bytes 786464 | tf_op jit(solution)/shard_map/ppermute | solution.py:384
  34.7 25.3 %conditional.1 = (f32[16,2,2,3,8,128]{5,4,3,2,1,0:T(8,128)S(1)}) conditional(s32[]{:T(128)} %bitcast.9, (s32[1]{0:T(128)}, s32[2,64]{1,0:T(2,128)S(1)}, f32[16,2,2,3,8,128]{5,4,3,2,1,0:T(8,128)S(1)}, f32[16,2,2,3,8,128]{5,4,3,2,1,0:T(8,128)S(1)}) %tuple.34, (s32[1]{0:T(128)}, s32[2,64]{1,0:T(2,128)S(1)}, ...), branch_computations={%region_0.0_spmd, %region_1.0_spmd, %region_2.0_spmd, %region_3.0_... | conditional | flops 125829120 | bytes 9437272 | solution.py:385
  34.7 0.8 outgoing.12
  35.4 6.2 %collective-permute-start.6 = (f32[14,2,3,8,128]{4,3,2,1,0:T(8,128)S(1)}, f32[14,2,3,8,128]{4,3,2,1,0:T(8,128)S(1)}, u32[]{:S(2)}, u32[]{:S(2)}) collective-permute-start(f32[14,2,3,8,128]{4,3,2,1,0:T(8,128)S(1)} %outgoing.12), channel_id=1, source_target_pairs={{0,8},{8,0},{1,9},{9,1},{2,10},{10,2},{3,11},{11,3},{4,12},{12,4},... | collective-permute-start | bytes 1032200 | tf_op jit(solution)/shard_map/cond/branch_3_fun/ppermute | solution.py:347
  41.6 15.6 %collective-permute-done.6.crossed_ref = f32[14,2,3,8,128]{4,3,2,1,0:T(8,128)S(1)} collective-permute-done((f32[14,2,3,8,128]{4,3,2,1,0:T(8,128)S(1)}, f32[14,2,3,8,128]{4,3,2,1,0:T(8,128)S(1)}, u32[]{:S(2)}, u32[]{:S(2)}) %collective-permute-start.6) | collective-permute-done | bytes 344096 | tf_op jit(solution)/shard_map/cond/branch_3_fun/ppermute | solution.py:347
  57.2 0.0 collective-permute-start.7
  57.2 1.6 %collective-permute-done.7.crossed_other_ref = f32[14,2,3,8,128]{4,3,2,1,0:T(8,128)S(1)} collective-permute-done((f32[14,2,3,8,128]{4,3,2,1,0:T(8,128)S(1)}, f32[14,2,3,8,128]{4,3,2,1,0:T(8,128)S(1)}, u32[]{:S(2)}, u32[]{:S(2)}) %collective-permute-start.7) | collective-permute-done | bytes 344096 | tf_op jit(solution)/shard_map/cond/branch_3_fun/ppermute | solution.py:348
  58.8 0.9 %slots.12 = f32[16,2,2,3,8,128]{5,4,3,2,1,0:T(8,128)S(1)} custom-call(s32[1]{0:T(128)} %get-tuple-element.99.core_ref, s32[2,64]{1,0:T(2,128)S(1)} %get-tuple-element.100.plan_ref, f32[16,2,2,3,8,128]{5,4,3,2,1,0:T(8,128)S(1)} %get-tuple-element.101.own_ref, f32[16,2,2,3,8,128]{5,4,3,2,1,0:T(8,128)S(1)} %get-tuple-element.102.other_ref, ...), custom_call_target="tpu_custom_call" | custom-call | flops 83886080 | bytes 2097152 | tf_op jit(solution)/shard_map/cond/branch_3_fun/slots/pallas_call | solution.py:349
  59.9 17.6 %all_to_all.11 = f32[16,2,2,3,8,128]{5,4,3,2,1,0:T(8,128)S(1)} all-to-all(f32[16,2,2,3,8,128]{5,4,3,2,1,0:T(8,128)S(1)} %get-tuple-element.137), channel_id=1, replica_groups=mesh['y'=4,'x'=4,'zh'=2,'core'=2,'row'=4] {'y','x'}, dimensions={0} | all-to-all | bytes 1572864 | tf_op jit(solution)/shard_map/all_to_all | solution.py:388
  77.5 0.9 %place.1 = f32[3,1,16,4096]{3,2,1,0:T(8,128)} custom-call(f32[32,2,3,8,128]{4,3,2,1,0:T(8,128)S(1)} %bitcast.13), custom_call_target="tpu_custom_call" | custom-call | flops 83886080 | bytes 2097152 | tf_op jit(solution)/shard_map/place/pallas_call | solution.py:360
Async XLA Ops:
  0.0 8.4 %copy-start.1 = (f32[16,4096]{1,0:T(8,128)S(1)}, f32[16,4096]{1,0:T(8,128)}, u32[]{:S(2)}) copy-start(f32[16,4096]{1,0:T(8,128)} %ground_ref.3) | copy-start | bytes 786436
  0.0 8.4 %copy-start = (f32[3,1,16,4096]{3,2,1,0:T(8,128)S(1)}, f32[3,1,16,4096]{3,2,1,0:T(8,128)}, u32[]{:S(2)}) copy-start(f32[3,1,16,4096]{3,2,1,0:T(8,128)} %state_ref.3) | copy-start | bytes 2359300
  1.0 10.3 %collective-permute-start.19 = (f32[4,1,4096]{2,1,0:T(1,128)S(1)}, f32[4,1,4096]{2,1,0:T(1,128)S(1)}, u32[]{:S(2)}, u32[]{:S(2)}) collective-permute-start(f32[4,1,4096]{2,1,0:T(1,128)S(1)} %get-tuple-element.130), channel_id=1, source_target_pairs={{1,0},{2,1},{3,2},{5,4},{6,5},{7,6},{9,8},{10,9},{11,10},{13,12},{... | collective-permute-start | bytes 196616 | tf_op jit(solution)/shard_map/ppermute | solution.py:307
  4.7 6.6 %collective-permute-start.18 = (f32[4,1,4096]{2,1,0:T(1,128)S(1)}, f32[4,1,4096]{2,1,0:T(1,128)S(1)}, u32[]{:S(2)}, u32[]{:S(2)}) collective-permute-start(f32[4,1,4096]{2,1,0:T(1,128)S(1)} %get-tuple-element.131), channel_id=1, source_target_pairs={{0,1},{1,2},{2,3},{4,5},{5,6},{6,7},{8,9},{9,10},{10,11},{12,13},{... | collective-permute-start | bytes 196616 | tf_op jit(solution)/shard_map/ppermute | solution.py:306
  6.9 0.7 copy-start.3
  6.9 0.7 copy-start.4
  8.4 1.0 %copy-start.2 = (f32[1,16,4096]{2,1,0:T(8,128)S(1)}, f32[1,16,4096]{2,1,0:T(8,128)}, u32[]{:S(2)}) copy-start(f32[1,16,4096]{2,1,0:T(8,128)} %rain_ref.1) | copy-start | bytes 786436
  32.4 2.3 %collective-permute-start.20 = (f32[16,2,2,3,8,128]{5,4,3,2,1,0:T(8,128)S(1)}, f32[16,2,2,3,8,128]{5,4,3,2,1,0:T(8,128)S(1)}, u32[]{:S(2)}, u32[]{:S(2)}) collective-permute-start(f32[16,2,2,3,8,128]{5,4,3,2,1,0:T(8,128)S(1)} %all_to_all.10), channel_id=1, source_target_pairs={{0,4},{4,0},{1,5},{5,1},{2,6},{6,2},{3,7},{7,3},{8,12},{12,8},{9,1... | collective-permute-start | bytes 2359304 | tf_op jit(solution)/shard_map/ppermute | solution.py:384
  35.4 21.8 %collective-permute-start.6 = (f32[14,2,3,8,128]{4,3,2,1,0:T(8,128)S(1)}, f32[14,2,3,8,128]{4,3,2,1,0:T(8,128)S(1)}, u32[]{:S(2)}, u32[]{:S(2)}) collective-permute-start(f32[14,2,3,8,128]{4,3,2,1,0:T(8,128)S(1)} %outgoing.12), channel_id=1, source_target_pairs={{0,8},{8,0},{1,9},{9,1},{2,10},{10,2},{3,11},{11,3},{4,12},{12,4},... | collective-permute-start | bytes 1032200 | tf_op jit(solution)/shard_map/cond/branch_3_fun/ppermute | solution.py:347
  57.2 1.7 %collective-permute-start.7 = (f32[14,2,3,8,128]{4,3,2,1,0:T(8,128)S(1)}, f32[14,2,3,8,128]{4,3,2,1,0:T(8,128)S(1)}, u32[]{:S(2)}, u32[]{:S(2)}) collective-permute-start(f32[14,2,3,8,128]{4,3,2,1,0:T(8,128)S(1)} %collective-permute-done.6.crossed_ref), channel_id=1, source_target_pairs={{0,4},{4,0},{1,5},{5,1},{2,6},{6,2},{3,7},{7,3},{8,12},{12,8},{9,1... | collective-permute-start | bytes 1032200 | tf_op jit(solution)/shard_map/cond/branch_3_fun/ppermute | solution.py:348
